TPU v7x, 32 devices: a whole 2x2x4 slice. The times are simulated.
32 devices in a mesh: layer: 2 (over y), unit: 8 (over z, x), feat: 2 (over core).
Axes of the slice: x: 2, y: 2, z: 4, core: 2. Of those that a mesh axis runs over, the one named last changes fastest.
Arguments:
- units: bfloat16 [57344, 24576], P(('layer', 'unit'), 'feat'), parts along dimension 0, may hold values from -1 to 1
- assign: int32 [57344], P(('layer', 'unit')), parts along dimension 0, may hold values from 0 to 511, as said below
- panel_idx: int32 [1024], P(('layer', 'unit')), parts along dimension 0, may hold values from 0 to 28671, as said below
Outputs:
- distances: float32 [1024, 512], P(('layer', 'unit'), 'feat'), parts along dimension 0
There are 2 independent parts, one for each index of `layer`. A program takes and returns all parts, laid end to end along the dimension named above; each array names one. Nothing has to cross between parts.
Inputs may be any that keep to these rules, and one draw needn't show every extreme that they name: `assign`: in each aligned block of 3584 entries, at most 896 name centroids of one owner (centroid // 64), and in every block some owner is named exactly 896 times. `panel_idx`: the entries of each aligned block of 64 index units of the matching aligned block of 3584 units.
All inputs are finite; a program needn't handle non-finite values.
Results may differ from a plain program's by a relative error of at most 0.0003.
Values may be sent and summed in bfloat16 or wider, within the bound.
A program may use at most 192 MiB of HBM per device.

v0:
```python
import jax
import jax.numpy as jnp
from jax import lax
from jax.sharding import PartitionSpec as P

CENT_DEV = 64


def shards(units, assign, panel_idx):
    unit_rows = units.shape[0]
    owners = lax.axis_size("unit")
    cent_dev = CENT_DEV
    all_cents = cent_dev * owners
    my_index = lax.axis_index("unit")
    cent_ids = lax.iota(jnp.int32, cent_dev * lax.axis_size("unit"))
    member = (cent_ids[:, None] == assign[None, :]).astype(jnp.bfloat16)
    cent_sums = lax.psum_scatter(
        jnp.dot(member, units, preferred_element_type=jnp.float32).astype(jnp.bfloat16),
        "unit",
        scatter_dimension=0,
        tiled=True,
    ).astype(jnp.float32)
    histogram = jnp.sum(
        (assign[:, None] == lax.iota(jnp.int32, all_cents)[None, :]).astype(jnp.float32), axis=0
    )
    totals = lax.psum(histogram, "unit")
    counts = lax.dynamic_slice_in_dim(totals, my_index * cent_dev, cent_dev)
    centroids = (cent_sums / jnp.maximum(counts, 1.0)[:, None]).astype(jnp.bfloat16)
    local_rows = panel_idx - my_index * unit_rows
    panel_rows = jnp.take(units, local_rows, axis=0)
    panel_float = panel_rows.astype(jnp.float32)
    panel_norms = jnp.sum(panel_float * panel_float, axis=1)
    pieces = lax.all_gather(centroids, "unit", axis=0, tiled=True)
    cent_float = pieces.astype(jnp.float32)
    cent_norms = jnp.sum(cent_float * cent_float, axis=1)
    inner_block = lax.dot_general(
        panel_rows, pieces, (((1,), (1,)), ((), ())), preferred_element_type=jnp.float32
    )
    block_terms = panel_norms[:, None] + cent_norms[None, :] - 2.0 * inner_block
    return lax.psum_scatter(block_terms, "feat", scatter_dimension=1, tiled=True)


def solution(mesh):
    in_specs = (P(("layer", "unit"), "feat"), P(("layer", "unit")), P(("layer", "unit")))
    out_specs = P(("layer", "unit"), "feat")
    return jax.shard_map(shards, mesh=mesh, in_specs=in_specs, out_specs=out_specs, check_vma=False)
```

profile of v0, /device:TPU:0, one launch (start us, length us, event | category | flops | bytes accessed | tf_op | source)
XLA Modules:
  0.0 477.4 jit_solution(8367983760903552789)
XLA Ops:
  6.5 0.0 reduce-scatter.3.cloned.1.call-start
  6.5 53.0 %convolution_convert_fusion = bf16[512,12288]{1,0:T(8,128)(2,1)} fusion(bf16[3584,12288]{1,0:T(8,128)(2,1)} %param.3, s32[3584]{0:T(1024)} %param.4), kind=kOutput, calls=%fused_computation.2 | convolution fusion | flops 45105283072 | bytes 100677632 | tf_op jit(solution)/shard_map/dot_general | solution.py:18
  59.5 0.0 copy-start.1
  59.5 0.0 reduce-scatter.3.cloned.1.call-update
  59.5 0.0 copy-start
  59.5 0.0 all-gather.2.cloned.1.call-start
  59.6 0.6 copy-done.1
  60.2 1.6 convert_reduce_fusion
  61.8 23.7 %psum.7 = f32[512]{0:T(512)S(1)} all-reduce(f32[512]{0:T(512)S(1)} %convert_reduce_fusion), channel_id=1, replica_groups=mesh['layer'=2,'unit'=8,'feat'=2] {'unit'}, use_global_device_ids=true, to_apply=%region_3.4 | all-reduce | flops 512 | bytes 4096 | tf_op jit(solution)/shard_map/psum | solution.py:26
  85.5 0.1 dynamic-slice_maximum_fusion
  85.6 184.4 %reduce-scatter.3.cloned.1.call-done = bf16[64,12288]{1,0:T(8,128)(2,1)} async-done(((bf16[512,12288]{1,0:T(8,128)(2,1)}), bf16[64,12288]{1,0:T(8,128)(2,1)}) %reduce-scatter.3.cloned.1.call-update) | async-done | bytes 1572880 | tf_op jit(solution)/shard_map/reduce_scatter | solution.py:17
  270.0 3.0 divide_convert_fusion
  272.9 0.0 all-gather.2.cloned.1.call-update
  273.0 0.2 reduce-scatter.5.cloned.1.call-start
  273.2 0.0 copy-done
  273.2 4.8 gather_fusion
  278.0 0.6 multiply_reduce_fusion.1
  278.6 170.1 %all-gather.2.cloned.1.call-done = bf16[512,12288]{1,0:T(8,128)(2,1)} async-done(((bf16[64,12288]{1,0:T(8,128)(2,1)}), bf16[512,12288]{1,0:T(8,128)(2,1)}) %all-gather.2.cloned.1.call-update) | async-done | bytes 12582928 | tf_op jit(solution)/shard_map/all_gather | solution.py:33
  448.7 7.1 %multiply_reduce_fusion = f32[512]{0:T(512)S(1)} fusion(bf16[512,12288]{1,0:T(8,128)(2,1)} %all-gather.2.cloned.1.call-done), kind=kLoop, calls=%fused_computation.1 | loop fusion | flops 18873856 | bytes 12584960 | tf_op jit(solution)/shard_map/reduce_sum | solution.py:35
  455.8 9.2 %fusion.1 = f32[64,512]{1,0:T(8,128)} fusion(bf16[512,12288]{1,0:T(8,128)(2,1)} %all-gather.2.cloned.1.call-done, bf16[64,12288]{1,0:T(8,128)(2,1)S(1)} %gather_fusion, pred[64]{0:T(512)(128)(4,1)S(1)} %get-tuple-element.5, f32[512]{0:T(512)S(1)} %multiply_reduce_fusion, f32[64]{0:T(128)S(1)} %multiply_reduce_fusion.1), kind=kOutput, calls=%fused_computation.11 | convolution fusion | flops 806191104 | bytes 14289216 | tf_op jit(solution)/shard_map/dot_general | solution.py:36
  465.0 0.0 reduce-scatter.5.cloned.1.call-update
  465.0 5.8 %reduce-scatter.5.cloned.1.call-done = f32[64,256]{1,0:T(8,128)} async-done(((f32[64,512]{1,0:T(8,128)}), f32[64,256]{1,0:T(8,128)}) %reduce-scatter.5.cloned.1.call-update) | async-done | bytes 65552 | tf_op jit(solution)/shard_map/reduce_scatter | solution.py:40
  (2 shorter events, 0.0 us)
Async XLA Ops:
  6.5 263.5 %reduce-scatter.3.cloned.1.call-start = ((), (), s32[]{:S(2)}) async-start(), calls=%async_computation.2 | async-start | bytes 14155776 | tf_op jit(solution)/shard_map/reduce_scatter | solution.py:17
  59.5 0.7 copy-start.1
  59.5 213.7 %copy-start = (s32[64]{0:T(128)S(1)}, s32[64]{0:T(128)}, u32[]{:S(2)}) copy-start(s32[64]{0:T(128)} %param.5) | copy-start | bytes 772
  59.5 389.1 %all-gather.2.cloned.1.call-start = ((), (), s32[]{:S(2)}) async-start(), calls=%async_computation.3 | async-start | bytes 14155776 | tf_op jit(solution)/shard_map/all_gather | solution.py:33
  273.0 197.9 %reduce-scatter.5.cloned.1.call-start = ((), (), s32[]{:S(2)}) async-start(), calls=%async_computation.4 | async-start | bytes 196608 | tf_op jit(solution)/shard_map/reduce_scatter | solution.py:40
Sparse Core Ops, SparseCore 0:
  59.6 210.2 reduce-scatter.2
  273.1 175.5 all-gather.1
  465.1 5.6 reduce-scatter.4
where the time goes:
time: 478 us; the launch traced here: 477 us
  waiting for transfers between devices  360 us (75%)
  matrix products  62.2 us (13%)
  blocking collectives  23.7 us (5%)
  between operations  13.2 us (3%)
  other arithmetic  12.3 us (3%)
  local copies, waits for them, and re-layouts  5.39 us (1%)
    reduce_scatter x1, waiting for transfers between devices, shards(): lax.psum_scatter(jnp.dot(member, units, preferred_element_type=jnp.float3...  184 us
    all_gather x1, waiting for transfers between devices, shards(): pieces = lax.all_gather(centroids, 'unit', axis=0, tiled=True)  170 us
    dot_general x1, matrix products, shards(): jnp.dot(member, units, preferred_element_type=jnp.float32)  53 us
    psum x1, blocking collectives, shards(): totals = lax.psum(histogram, 'unit')  23.7 us
  transfers between devices with their start and end apart: 3, of which 3 were waited for; matrix products, arithmetic and copies ran while one was open for 1% of the time, Pallas kernels for 0%

commit v1 on v0

--- a/solution.py
+++ b/solution.py
@@ -1,9 +1,324 @@
+import functools
+
 import jax
 import jax.numpy as jnp
 from jax import lax
+from jax.experimental import pallas as pl
+from jax.experimental.pallas import tpu as pltpu
 from jax.sharding import PartitionSpec as P
 
 CENT_DEV = 64
+PIECE = 256
+LAG = 4
+MESH = pl.DeviceIdType.MESH
+NT = (((1,), (1,)), ((), ()))
+
+
+def group_quarter(z, g):
+    inner = jnp.where(g == 0, 3, jnp.where(g == 1, 0, jnp.where(g == 2, 2, 1)))
+    outer = 3 - g
+    near = jnp.where((z == 0) | (z == 3), outer, inner)
+    return jnp.where(z < 2, near, 3 - near)
+
+
+def kernel(
+    subs, panel_dev,
+    assign_ref, panel_ref, units_ref, out_ref,
+    member, ubuf, xsend, own, xrecv, urecv, drecv, acc, fin,
+    psend, precv, hist, hrecv, gram, norm, pnorm, dhalf, frecv, esum, erecv,
+    usem, xs_sem, xr_sem, zs_sem, ur_sem, dr_sem,
+    ps_sem, pr_sem, hs_sem, hr_sem, f_sem, es_sem, er_sem,
+):
+    me = lax.axis_index("unit")
+    feat = lax.axis_index("feat")
+    z, x = me // 2, me % 2
+    mate = me + 1 - 2 * x
+    cents = own.shape[1]
+    rows = units_ref.shape[0]
+    pieces = 4 * subs
+
+    barrier = pltpu.get_barrier_semaphore()
+    for d in range(1, 8):
+        pl.semaphore_signal(
+            barrier, inc=1, device_id={"unit": (me + d) % 8}, device_id_type=MESH
+        )
+    pl.semaphore_signal(barrier, inc=1, device_id={"feat": 1 - feat}, device_id_type=MESH)
+
+    def fetch(t):
+        i, h = t // 2, t % 2
+        q = group_quarter(z, i // subs)
+        side = jnp.where(h == 0, 1 - x, x)
+        start = ((side * 4 + q) * subs + i % subs) * PIECE
+        return pltpu.make_async_copy(
+            units_ref.at[:, pl.ds(pl.multiple_of(start, PIECE), PIECE)],
+            ubuf.at[t % 3],
+            usem.at[t % 3],
+        )
+
+    fetch(0).start()
+    fetch(1).start()
+
+    def build(b, carry):
+        first = pl.multiple_of(b * 64, 64)
+        ids = lax.broadcasted_iota(jnp.int32, (64, rows), 0) + first
+        member[pl.ds(first, 64), :] = jnp.where(ids == assign_ref[...], 1.0, 0.0).astype(jnp.bfloat16)
+        return carry
+
+    lax.fori_loop(0, cents // 64, build, 0)
+    unit_ids = lax.broadcasted_iota(jnp.int32, (panel_dev, rows), 1)
+    member[cents : cents + panel_dev, :] = jnp.where(unit_ids == panel_ref[...], 1.0, 0.0).astype(jnp.bfloat16)
+
+    def x_copy(i):
+        return pltpu.make_async_remote_copy(
+            src_ref=xsend.at[i], dst_ref=xrecv.at[i], send_sem=xs_sem.at[i], recv_sem=xr_sem.at[i],
+            device_id={"unit": mate}, device_id_type=MESH,
+        )
+
+    def up_copy(i, slot):
+        return pltpu.make_async_remote_copy(
+            src_ref=own.at[i], dst_ref=urecv.at[slot], send_sem=zs_sem.at[i], recv_sem=ur_sem.at[slot],
+            device_id={"unit": (me + 2) % 8}, device_id_type=MESH,
+        )
+
+    def down_copy(i, slot):
+        return pltpu.make_async_remote_copy(
+            src_ref=own.at[i], dst_ref=drecv.at[slot], send_sem=zs_sem.at[i], recv_sem=dr_sem.at[slot],
+            device_id={"unit": (me + 6) % 8}, device_id_type=MESH,
+        )
+
+    def panel_copy(to, source):
+        return pltpu.make_async_remote_copy(
+            src_ref=psend.at[to], dst_ref=precv.at[:, pl.ds(pl.multiple_of(source * panel_dev, panel_dev), panel_dev), :],
+            send_sem=ps_sem.at[to], recv_sem=pr_sem.at[source],
+            device_id={"unit": to}, device_id_type=MESH,
+        )
+
+    def hist_copy(to, source):
+        return pltpu.make_async_remote_copy(
+            src_ref=hist, dst_ref=hrecv.at[source], send_sem=hs_sem.at[to], recv_sem=hr_sem.at[source],
+            device_id={"unit": to}, device_id_type=MESH,
+        )
+
+    def sum_copy(to, source):
+        return pltpu.make_async_remote_copy(
+            src_ref=esum.at[pl.ds(pl.multiple_of(to * panel_dev, panel_dev), panel_dev), :], dst_ref=erecv.at[source],
+            send_sem=es_sem.at[to], recv_sem=er_sem.at[source],
+            device_id={"unit": to}, device_id_type=MESH,
+        )
+
+    pl.semaphore_wait(barrier, 8)
+
+    def compute(t, carry):
+        i, h = t // 2, t % 2
+        q, s = group_quarter(z, i // subs), i % subs
+        side = jnp.where(h == 0, 1 - x, x)
+        to = 2 * q + side
+
+        @pl.when(t + 2 < 2 * pieces)
+        def _():
+            fetch(t + 2).start()
+
+        fetch(t).wait()
+        part = jnp.dot(member[...], ubuf[t % 3], preferred_element_type=jnp.float32).astype(jnp.bfloat16)
+
+        @pl.when(h == 0)
+        def _():
+            xsend[i] = part[:cents]
+            x_copy(i).start()
+
+        @pl.when(h == 1)
+        def _():
+            own[i] = part[:cents]
+
+        @pl.when(to == me)
+        def _():
+            precv[s, pl.ds(pl.multiple_of(me * panel_dev, panel_dev), panel_dev), :] = part[cents:]
+
+        @pl.when(to != me)
+        def _():
+            psend[to, s] = part[cents:]
+
+            @pl.when(s == subs - 1)
+            def _():
+                panel_copy(to, me).start()
+
+        return carry
+
+    def reduce(i):
+        q, s = group_quarter(z, i // subs), i % subs
+        slot = q * subs + s
+        x_copy(i).wait_recv()
+        acc[...] = own[i].astype(jnp.float32) + xrecv[i].astype(jnp.float32)
+
+        @pl.when((z > 0) & (q >= z))
+        def _():
+            up_copy(i, slot).wait_recv()
+            acc[...] += urecv[slot].astype(jnp.float32)
+
+        @pl.when((z < 3) & (q <= z))
+        def _():
+            down_copy(i, slot).wait_recv()
+            acc[...] += drecv[slot].astype(jnp.float32)
+
+        @pl.when(q > z)
+        def _():
+            own[i] = acc[...].astype(jnp.bfloat16)
+            up_copy(i, slot).start()
+
+        @pl.when(q < z)
+        def _():
+            own[i] = acc[...].astype(jnp.bfloat16)
+            down_copy(i, slot).start()
+
+        @pl.when(q == z)
+        def _():
+            fin[s] = acc[...].astype(jnp.bfloat16)
+
+    def step(i, carry):
+        @pl.when(i < pieces)
+        def _():
+            lax.fori_loop(2 * i, 2 * i + 2, compute, 0)
+
+        @pl.when(i == 2)
+        def _():
+            ones = jnp.ones((8, rows), jnp.bfloat16)
+            hist[...] = lax.dot_general(ones, member[:cents, :], NT, preferred_element_type=jnp.float32)
+            hrecv[me] = hist[...]
+            for d in range(1, 8):
+                hist_copy((me + d) % 8, me).start()
+
+        @pl.when(i >= LAG)
+        def _():
+            reduce(i - LAG)
+
+        return carry
+
+    lax.fori_loop(0, pieces + LAG, step, 0)
+
+    for d in range(1, 8):
+        source = (me + d) % 8
+        hist_copy(source, source).wait_recv()
+        panel_copy(source, source).wait_recv()
+
+    gram[...] = jnp.zeros_like(gram)
+    norm[...] = jnp.zeros_like(norm)
+    pnorm[...] = jnp.zeros_like(pnorm)
+
+    def finish(s, carry):
+        panel, cent = precv[s], fin[s]
+        gram[...] += lax.dot_general(panel, cent, NT, preferred_element_type=jnp.float32)
+        wide = cent.astype(jnp.float32)
+        square = wide * wide
+        high = square.astype(jnp.bfloat16)
+        low = (square - high.astype(jnp.float32)).astype(jnp.bfloat16)
+        ones = jnp.ones((8, PIECE), jnp.bfloat16)
+        norm[...] += lax.dot_general(ones, high, NT, preferred_element_type=jnp.float32)
+        norm[...] += lax.dot_general(ones, low, NT, preferred_element_type=jnp.float32)
+        panel_wide = panel.astype(jnp.float32)
+        panel_square = panel_wide * panel_wide
+        pnorm[...] += panel_square[:, :128] + panel_square[:, 128:]
+        return carry
+
+    lax.fori_loop(0, subs, finish, 0)
+
+    counts = hrecv[0][0:1, :]
+    for v in range(1, 8):
+        counts = counts + hrecv[v][0:1, :]
+    inverse = 1.0 / jnp.maximum(counts, 1.0)
+    cent_norm = norm[0:1, :] * inverse * inverse
+    panel_norm = jnp.sum(pnorm[...], axis=1, keepdims=True)
+    half = cents // 2
+    for h in range(2):
+        lanes = slice(h * half, (h + 1) * half)
+        dhalf[h] = panel_norm + cent_norm[:, lanes] - 2.0 * (gram[:, lanes] * inverse[:, lanes])
+    swap = pltpu.make_async_remote_copy(
+        src_ref=dhalf.at[1 - feat], dst_ref=frecv, send_sem=f_sem.at[0], recv_sem=f_sem.at[1],
+        device_id={"feat": 1 - feat}, device_id_type=MESH,
+    )
+    swap.start()
+    swap.wait_recv()
+    esum[...] = dhalf[feat] + frecv[...]
+    for d in range(1, 8):
+        sum_copy((me + d) % 8, me).start()
+    erecv[me] = esum[pl.ds(pl.multiple_of(me * panel_dev, panel_dev), panel_dev), :]
+    for d in range(1, 8):
+        source = (me + d) % 8
+        sum_copy(source, source).wait_recv()
+    total = erecv[0]
+    for v in range(1, 8):
+        total = total + erecv[v]
+    out_ref[...] = total
+
+    swap.wait_send()
+    for d in range(1, 8):
+        to = (me + d) % 8
+        hist_copy(to, me).wait_send()
+        panel_copy(to, me).wait_send()
+        sum_copy(to, me).wait_send()
+
+    def drain(i, carry):
+        x_copy(i).wait_send()
+        q = group_quarter(z, i // subs)
+
+        @pl.when(q > z)
+        def _():
+            up_copy(i, q * subs + i % subs).wait_send()
+
+        @pl.when(q < z)
+        def _():
+            down_copy(i, q * subs + i % subs).wait_send()
+
+        return carry
+
+    lax.fori_loop(0, pieces, drain, 0)
+
+
+def fused_shards(units, assign, panel_idx):
+    rows, features = units.shape
+    panel_dev = panel_idx.shape[0]
+    cents = CENT_DEV * 8
+    subs = features // (8 * PIECE)
+    pieces = 4 * subs
+    local_rows = panel_idx - lax.axis_index("unit") * rows
+    bf16, f32, dma = jnp.bfloat16, jnp.float32, pltpu.SemaphoreType.DMA
+    panel = 8 * panel_dev
+    half = cents // 2
+    block = pltpu.VMEM((pieces, cents, PIECE), bf16)
+    vmem = pl.BlockSpec(memory_space=pltpu.VMEM)
+    return pl.pallas_call(
+        functools.partial(kernel, subs, panel_dev),
+        out_shape=jax.ShapeDtypeStruct((panel_dev, half), f32),
+        in_specs=[vmem, vmem, pl.BlockSpec(memory_space=pl.ANY)],
+        out_specs=vmem,
+        scratch_shapes=[
+            pltpu.VMEM((cents + panel_dev, rows), bf16),
+            pltpu.VMEM((3, rows, PIECE), bf16),
+            block, block, block, block, block,
+            pltpu.VMEM((cents, PIECE), f32),
+            pltpu.VMEM((subs, cents, PIECE), bf16),
+            pltpu.VMEM((8, subs, panel_dev, PIECE), bf16),
+            pltpu.VMEM((subs, panel, PIECE), bf16),
+            pltpu.VMEM((8, cents), f32),
+            pltpu.VMEM((8, 8, cents), f32),
+            pltpu.VMEM((panel, cents), f32),
+            pltpu.VMEM((8, cents), f32),
+            pltpu.VMEM((panel, 128), f32),
+            pltpu.VMEM((2, panel, half), f32),
+            pltpu.VMEM((panel, half), f32),
+            pltpu.VMEM((panel, half), f32),
+            pltpu.VMEM((8, panel_dev, half), f32),
+            dma((3,)), dma((pieces,)), dma((pieces,)), dma((pieces,)), dma((pieces,)), dma((pieces,)),
+            dma((8,)), dma((8,)), dma((8,)), dma((8,)), dma((2,)), dma((8,)), dma((8,)),
+        ],
+        cost_estimate=pl.CostEstimate(
+            flops=2 * (cents + panel_dev) * rows * features,
+            bytes_accessed=2 * rows * features,
+            transcendentals=0,
+        ),
+        compiler_params=pltpu.CompilerParams(
+            collective_id=0, has_side_effects=True, vmem_limit_bytes=60 * 1024 * 1024
+        ),
+    )(assign.reshape(1, rows), local_rows.reshape(panel_dev, 1), units)
 
 
 def shards(units, assign, panel_idx):
@@ -43,4 +358,6 @@
 def solution(mesh):
     in_specs = (P(("layer", "unit"), "feat"), P(("layer", "unit")), P(("layer", "unit")))
     out_specs = P(("layer", "unit"), "feat")
-    return jax.shard_map(shards, mesh=mesh, in_specs=in_specs, out_specs=out_specs, check_vma=False)
+    fused = mesh.shape["unit"] == 8 and mesh.shape["feat"] == 2
+    body = fused_shards if fused else shards
+    return jax.shard_map(body, mesh=mesh, in_specs=in_specs, out_specs=out_specs, check_vma=False)

time: 478 us -> 184 us (0.38)
  waiting for transfers between devices: 360 us -> 0 us
  Pallas kernels: 0 us -> 177 us
  matrix products: 62.2 us -> 0 us
  blocking collectives: 23.7 us -> 0 us
  between operations: 13.2 us -> 0.01 us
  other arithmetic: 12.3 us -> 0.66 us
    reduce_scatter x2 -> x0, waiting for transfers between devices: 190 us -> none  [the longest x1 184 us: shards(): lax.psum_scatter(jnp.dot(member, units, preferred_element_type=jnp.float3...]
    pallas_call x0 -> x1, Pallas kernels: none -> 177 us  [fused_shards(): pl.pallas_call(functools.partial(kernel, subs, panel_dev), out_shape=jax....]
    all_gather x1 -> x0, waiting for transfers between devices: 170 us -> none  [shards(): pieces = lax.all_gather(centroids, 'unit', axis=0, tiled=True)]
    dot_general x2 -> x0, matrix products: 62.2 us -> none  [the longest x1 53 us: shards(): jnp.dot(member, units, preferred_element_type=jnp.float32)]
    psum x1 -> x0, blocking collectives: 23.7 us -> none  [shards(): totals = lax.psum(histogram, 'unit')]
    reduce_sum x3 -> x0, other arithmetic: 9.29 us -> none  [the longest x1 7.12 us: shards(): cent_norms = jnp.sum(cent_float * cent_float, axis=1)]
  transfers between devices with their start and end apart: 3 -> 0, of which waited for: 3 -> 0; matrix products, arithmetic and copies ran while one was open for 1% -> 0% of each run, Pallas kernels for 0% -> 0%
where the time goes in v1:
time: 184 us; the launch traced here: 181 us
  Pallas kernels  177 us (96%)
  local copies, waits for them, and re-layouts  3.51 us (2%)
    pallas_call x1, Pallas kernels, fused_shards(): pl.pallas_call(functools.partial(kernel, subs, panel_dev), out_shape=jax....  177 us

profile of v1, /device:TPU:0, one launch (start us, length us, event | category | flops | bytes accessed | tf_op | source)
XLA Modules:
  0.0 180.8 jit_solution(244779210684846882)
XLA Ops:
  0.0 0.7 subtract_bitcast_fusion
  0.7 1.3 reshape.6.assign_ref
  2.0 0.7 copy.4.panel_ref
  2.7 176.6 %shard_map.37 = f32[64,256]{1,0:T(8,128)} custom-call(s32[1,3584]{1,0:T(1,128)} %reshape.6.assign_ref, s32[64,1]{1,0:T(8,128)} %copy.4.panel_ref, bf16[3584,12288]{1,0:T(8,128)(2,1)} %units_ref.1), custom_call_target="tpu_custom_call" | custom-call | flops 50734301184 | bytes 88080384 | tf_op jit(solution)/shard_map/pallas_call | solution.py:288
  179.3 1.5 copy.6

commit v2 on v1

--- a/solution.py
+++ b/solution.py
@@ -9,7 +9,8 @@
 
 CENT_DEV = 64
 PIECE = 256
-LAG = 4
+LAG = 12
+END_LAG = 8
 MESH = pl.DeviceIdType.MESH
 NT = (((1,), (1,)), ((), ()))
 
@@ -21,13 +22,17 @@
     return jnp.where(z < 2, near, 3 - near)
 
 
+def z_first(q, s):
+    return (s == 1) & ((q == 0) | (q == 3))
+
+
 def kernel(
     subs, panel_dev,
     assign_ref, panel_ref, units_ref, out_ref,
-    member, ubuf, xsend, own, xrecv, urecv, drecv, acc, fin,
+    member, ubuf, xsend, own, xrecv, urecv, drecv, acc, macc, murecv, mdrecv,
     psend, precv, hist, hrecv, gram, norm, pnorm, dhalf, frecv, esum, erecv,
-    usem, xs_sem, xr_sem, zs_sem, ur_sem, dr_sem,
-    ps_sem, pr_sem, hs_sem, hr_sem, f_sem, es_sem, er_sem,
+    usem, xs_sem, xr_sem, zs_sem, ur_sem, dr_sem, ms_sem, mu_sem, md_sem,
+    ps_sem, pr_sem, hs_sem, hr_sem, fs_sem, fr_sem, es_sem, er_sem,
 ):
     me = lax.axis_index("unit")
     feat = lax.axis_index("feat")
@@ -36,6 +41,7 @@
     cents = own.shape[1]
     rows = units_ref.shape[0]
     pieces = 4 * subs
+    lag = jnp.where((z == 0) | (z == 3), END_LAG, LAG)
 
     barrier = pltpu.get_barrier_semaphore()
     for d in range(1, 8):
@@ -86,10 +92,23 @@
             device_id={"unit": (me + 6) % 8}, device_id_type=MESH,
         )
 
-    def panel_copy(to, source):
-        return pltpu.make_async_remote_copy(
-            src_ref=psend.at[to], dst_ref=precv.at[:, pl.ds(pl.multiple_of(source * panel_dev, panel_dev), panel_dev), :],
-            send_sem=ps_sem.at[to], recv_sem=pr_sem.at[source],
+    def mate_up_copy(i, q):
+        return pltpu.make_async_remote_copy(
+            src_ref=xsend.at[i], dst_ref=murecv.at[q], send_sem=ms_sem.at[q], recv_sem=mu_sem.at[q],
+            device_id={"unit": (me + 2) % 8}, device_id_type=MESH,
+        )
+
+    def mate_down_copy(i, q):
+        return pltpu.make_async_remote_copy(
+            src_ref=xsend.at[i], dst_ref=mdrecv.at[q], send_sem=ms_sem.at[q], recv_sem=md_sem.at[q],
+            device_id={"unit": (me + 6) % 8}, device_id_type=MESH,
+        )
+
+    def panel_copy(to, source, s):
+        return pltpu.make_async_remote_copy(
+            src_ref=psend.at[to, s],
+            dst_ref=precv.at[s, pl.ds(pl.multiple_of(source * panel_dev, panel_dev), panel_dev), :],
+            send_sem=ps_sem.at[to * subs + s], recv_sem=pr_sem.at[source * subs + s],
             device_id={"unit": to}, device_id_type=MESH,
         )
 
@@ -105,6 +124,10 @@
             send_sem=es_sem.at[to], recv_sem=er_sem.at[source],
             device_id={"unit": to}, device_id_type=MESH,
         )
+
+    gram[...] = jnp.zeros_like(gram)
+    norm[...] = jnp.zeros_like(norm)
+    pnorm[...] = jnp.zeros_like(pnorm)
 
     pl.semaphore_wait(barrier, 8)
 
@@ -124,7 +147,10 @@
         @pl.when(h == 0)
         def _():
             xsend[i] = part[:cents]
-            x_copy(i).start()
+
+            @pl.when(jnp.logical_not(z_first(q, s)))
+            def _():
+                x_copy(i).start()
 
         @pl.when(h == 1)
         def _():
@@ -137,75 +163,15 @@
         @pl.when(to != me)
         def _():
             psend[to, s] = part[cents:]
-
-            @pl.when(s == subs - 1)
-            def _():
-                panel_copy(to, me).start()
+            panel_copy(to, me, s).start()
 
         return carry
 
-    def reduce(i):
-        q, s = group_quarter(z, i // subs), i % subs
-        slot = q * subs + s
-        x_copy(i).wait_recv()
-        acc[...] = own[i].astype(jnp.float32) + xrecv[i].astype(jnp.float32)
-
-        @pl.when((z > 0) & (q >= z))
-        def _():
-            up_copy(i, slot).wait_recv()
-            acc[...] += urecv[slot].astype(jnp.float32)
-
-        @pl.when((z < 3) & (q <= z))
-        def _():
-            down_copy(i, slot).wait_recv()
-            acc[...] += drecv[slot].astype(jnp.float32)
-
-        @pl.when(q > z)
-        def _():
-            own[i] = acc[...].astype(jnp.bfloat16)
-            up_copy(i, slot).start()
-
-        @pl.when(q < z)
-        def _():
-            own[i] = acc[...].astype(jnp.bfloat16)
-            down_copy(i, slot).start()
-
-        @pl.when(q == z)
-        def _():
-            fin[s] = acc[...].astype(jnp.bfloat16)
-
-    def step(i, carry):
-        @pl.when(i < pieces)
-        def _():
-            lax.fori_loop(2 * i, 2 * i + 2, compute, 0)
-
-        @pl.when(i == 2)
-        def _():
-            ones = jnp.ones((8, rows), jnp.bfloat16)
-            hist[...] = lax.dot_general(ones, member[:cents, :], NT, preferred_element_type=jnp.float32)
-            hrecv[me] = hist[...]
-            for d in range(1, 8):
-                hist_copy((me + d) % 8, me).start()
-
-        @pl.when(i >= LAG)
-        def _():
-            reduce(i - LAG)
-
-        return carry
-
-    lax.fori_loop(0, pieces + LAG, step, 0)
-
-    for d in range(1, 8):
-        source = (me + d) % 8
-        hist_copy(source, source).wait_recv()
-        panel_copy(source, source).wait_recv()
-
-    gram[...] = jnp.zeros_like(gram)
-    norm[...] = jnp.zeros_like(norm)
-    pnorm[...] = jnp.zeros_like(pnorm)
-
-    def finish(s, carry):
-        panel, cent = precv[s], fin[s]
+    def finish(s):
+        for d in range(1, 8):
+            source = (me + d) % 8
+            panel_copy(source, source, s).wait_recv()
+        panel, cent = precv[s], acc[...].astype(jnp.bfloat16)
         gram[...] += lax.dot_general(panel, cent, NT, preferred_element_type=jnp.float32)
         wide = cent.astype(jnp.float32)
         square = wide * wide
@@ -217,9 +183,105 @@
         panel_wide = panel.astype(jnp.float32)
         panel_square = panel_wide * panel_wide
         pnorm[...] += panel_square[:, :128] + panel_square[:, 128:]
+
+    def reduce(i):
+        q, s = group_quarter(z, i // subs), i % subs
+        slot = q * subs + s
+        early = z_first(q, s)
+        acc[...] = own[i].astype(jnp.float32)
+
+        @pl.when(early)
+        def _():
+            macc[...] = xsend[i].astype(jnp.float32)
+
+        @pl.when(jnp.logical_not(early))
+        def _():
+            x_copy(i).wait_recv()
+            acc[...] += xrecv[i].astype(jnp.float32)
+
+        @pl.when((z > 0) & (q >= z))
+        def _():
+            up_copy(i, slot).wait_recv()
+            acc[...] += urecv[slot].astype(jnp.float32)
+
+            @pl.when(early)
+            def _():
+                mate_up_copy(i, q).wait_recv()
+                macc[...] += murecv[q].astype(jnp.float32)
+
+        @pl.when((z < 3) & (q <= z))
+        def _():
+            down_copy(i, slot).wait_recv()
+            acc[...] += drecv[slot].astype(jnp.float32)
+
+            @pl.when(early)
+            def _():
+                mate_down_copy(i, q).wait_recv()
+                macc[...] += mdrecv[q].astype(jnp.float32)
+
+        @pl.when(early)
+        def _():
+            xsend[i] = macc[...].astype(jnp.bfloat16)
+
+        @pl.when(early | (q != z))
+        def _():
+            own[i] = acc[...].astype(jnp.bfloat16)
+
+        @pl.when(q > z)
+        def _():
+            up_copy(i, slot).start()
+
+            @pl.when(early)
+            def _():
+                mate_up_copy(i, q).start()
+
+        @pl.when(q < z)
+        def _():
+            down_copy(i, slot).start()
+
+            @pl.when(early)
+            def _():
+                mate_down_copy(i, q).start()
+
+        @pl.when((q == z) & early)
+        def _():
+            x_copy(i).start()
+
+        @pl.when((q == z) & jnp.logical_not(early))
+        def _():
+            finish(s)
+
+    def step(i, carry):
+        @pl.when(i < pieces)
+        def _():
+            lax.fori_loop(2 * i, 2 * i + 2, compute, 0)
+
+        @pl.when(i == 2)
+        def _():
+            ones = jnp.ones((8, rows), jnp.bfloat16)
+            hist[...] = lax.dot_general(ones, member[:cents, :], NT, preferred_element_type=jnp.float32)
+            hrecv[me] = hist[...]
+            for d in range(1, 8):
+                hist_copy((me + d) % 8, me).start()
+
+        @pl.when((i >= lag) & (i < pieces + lag))
+        def _():
+            reduce(i - lag)
+
         return carry
 
-    lax.fori_loop(0, subs, finish, 0)
+    lax.fori_loop(0, pieces + LAG, step, 0)
+
+    @pl.when(z_first(z, 1))
+    def _():
+        last = 3 * subs + 1
+        x_copy(last).wait_recv()
+        acc[...] = own[last].astype(jnp.float32) + xrecv[last].astype(jnp.float32)
+        finish(1)
+
+    for d in range(1, 8):
+        source = (me + d) % 8
+        hist_copy(source, source).wait_recv()
 
     counts = hrecv[0][0:1, :]
     for v in range(1, 8):
@@ -231,16 +293,25 @@
     for h in range(2):
         lanes = slice(h * half, (h + 1) * half)
         dhalf[h] = panel_norm + cent_norm[:, lanes] - 2.0 * (gram[:, lanes] * inverse[:, lanes])
-    swap = pltpu.make_async_remote_copy(
-        src_ref=dhalf.at[1 - feat], dst_ref=frecv, send_sem=f_sem.at[0], recv_sem=f_sem.at[1],
-        device_id={"feat": 1 - feat}, device_id_type=MESH,
-    )
-    swap.start()
-    swap.wait_recv()
-    esum[...] = dhalf[feat] + frecv[...]
-    for d in range(1, 8):
-        sum_copy((me + d) % 8, me).start()
-    erecv[me] = esum[pl.ds(pl.multiple_of(me * panel_dev, panel_dev), panel_dev), :]
+    def swap_copy(v):
+        lines = pl.ds(pl.multiple_of(v * panel_dev, panel_dev), panel_dev)
+        return pltpu.make_async_remote_copy(
+            src_ref=dhalf.at[1 - feat, lines, :], dst_ref=frecv.at[lines, :],
+            send_sem=fs_sem.at[v], recv_sem=fr_sem.at[v],
+            device_id={"feat": 1 - feat}, device_id_type=MESH,
+        )
+
+    for d in range(1, 9):
+        swap_copy((me + d) % 8).start()
+    for d in range(1, 9):
+        to = (me + d) % 8
+        lines = pl.ds(pl.multiple_of(to * panel_dev, panel_dev), panel_dev)
+        swap_copy(to).wait_recv()
+        if d < 8:
+            esum[lines, :] = dhalf[feat, lines, :] + frecv[lines, :]
+            sum_copy(to, me).start()
+        else:
+            erecv[me] = dhalf[feat, lines, :] + frecv[lines, :]
     for d in range(1, 8):
         source = (me + d) % 8
         sum_copy(source, source).wait_recv()
@@ -249,24 +320,38 @@
         total = total + erecv[v]
     out_ref[...] = total
 
-    swap.wait_send()
+    for v in range(8):
+        swap_copy(v).wait_send()
     for d in range(1, 8):
         to = (me + d) % 8
         hist_copy(to, me).wait_send()
-        panel_copy(to, me).wait_send()
+        for s in range(subs):
+            panel_copy(to, me, s).wait_send()
         sum_copy(to, me).wait_send()
 
     def drain(i, carry):
-        x_copy(i).wait_send()
-        q = group_quarter(z, i // subs)
+        q, s = group_quarter(z, i // subs), i % subs
+        early = z_first(q, s)
+
+        @pl.when(jnp.logical_not(early) | (q == z))
+        def _():
+            x_copy(i).wait_send()
 
         @pl.when(q > z)
         def _():
-            up_copy(i, q * subs + i % subs).wait_send()
+            up_copy(i, q * subs + s).wait_send()
+
+            @pl.when(early)
+            def _():
+                mate_up_copy(i, q).wait_send()
 
         @pl.when(q < z)
         def _():
-            down_copy(i, q * subs + i % subs).wait_send()
+            down_copy(i, q * subs + s).wait_send()
+
+            @pl.when(early)
+            def _():
+                mate_down_copy(i, q).wait_send()
 
         return carry
 
@@ -294,8 +379,8 @@
             pltpu.VMEM((cents + panel_dev, rows), bf16),
             pltpu.VMEM((3, rows, PIECE), bf16),
             block, block, block, block, block,
-            pltpu.VMEM((cents, PIECE), f32),
-            pltpu.VMEM((subs, cents, PIECE), bf16),
+            pltpu.VMEM((cents, PIECE), f32), pltpu.VMEM((cents, PIECE), f32),
+            pltpu.VMEM((4, cents, PIECE), bf16), pltpu.VMEM((4, cents, PIECE), bf16),
             pltpu.VMEM((8, subs, panel_dev, PIECE), bf16),
             pltpu.VMEM((subs, panel, PIECE), bf16),
             pltpu.VMEM((8, cents), f32),
@@ -308,7 +393,8 @@
             pltpu.VMEM((panel, half), f32),
             pltpu.VMEM((8, panel_dev, half), f32),
             dma((3,)), dma((pieces,)), dma((pieces,)), dma((pieces,)), dma((pieces,)), dma((pieces,)),
-            dma((8,)), dma((8,)), dma((8,)), dma((8,)), dma((2,)), dma((8,)), dma((8,)),
+            dma((4,)), dma((4,)), dma((4,)),
+            dma((8 * subs,)), dma((8 * subs,)), dma((8,)), dma((8,)), dma((8,)), dma((8,)), dma((8,)), dma((8,)),
         ],
         cost_estimate=pl.CostEstimate(
             flops=2 * (cents + panel_dev) * rows * features,

time: 184 us -> 175 us (0.951); the launches traced: 181 us -> 174 us
  Pallas kernels: 177 us -> 170 us
    pallas_call x1, Pallas kernels: 177 us -> 170 us  [fused_shards(): pl.pallas_call(functools.partial(kernel, subs, panel_dev), out_shape=jax....]
where the time goes in v2:
time: 175 us; the launch traced here: 174 us
  Pallas kernels  170 us (97%)
  local copies, waits for them, and re-layouts  3.51 us (2%)
    pallas_call x1, Pallas kernels, fused_shards(): pl.pallas_call(functools.partial(kernel, subs, panel_dev), out_shape=jax....  170 us

profile of v2, /device:TPU:0, one launch (start us, length us, event | category | flops | bytes accessed | tf_op | source)
XLA Modules:
  0.0 174.2 jit_solution(9354940393036617879)
XLA Ops:
  0.0 0.7 subtract_bitcast_fusion
  0.7 1.3 reshape.6.assign_ref
  2.0 0.7 copy.4.panel_ref
  2.7 170.0 %shard_map.37 = f32[64,256]{1,0:T(8,128)} custom-call(s32[1,3584]{1,0:T(1,128)} %reshape.6.assign_ref, s32[64,1]{1,0:T(8,128)} %copy.4.panel_ref, bf16[3584,12288]{1,0:T(8,128)(2,1)} %units_ref.1), custom_call_target="tpu_custom_call" | custom-call | flops 50734301184 | bytes 88080384 | tf_op jit(solution)/shard_map/pallas_call | solution.py:373
  172.7 1.5 copy.6
